TPU v7x, 32 devices: a whole 2x2x4 slice. The times are simulated.
32 devices in a mesh: region: 2 (over y), gz: 4 (over z), shot: 2 (over x), gx: 2 (over core).
Axes of the slice: x: 2, y: 2, z: 4, core: 2. Of those that a mesh axis runs over, the one named last changes fastest.
Arguments:
- probes: float32 [64, 16, 16, 128], P(('region', 'gz'), 'gx'), parts along dimension 0, may hold values from -6 to 6
- speed: float32 [64, 16, 16], P(('region', 'gz'), 'gx'), parts along dimension 0, may hold values from 0.02 to 0.18
- incident: float32 [4, 32, 16, 16], P(('region', 'shot'), 'gz', 'gx'), parts along dimension 0, may hold values from -6 to 6
- wavelet: float32 [4, 6], P(('region', 'shot')), parts along dimension 0, may hold values from -1.2 to 1.2
- receivers: int32 [4, 64], P(('region', 'shot')), parts along dimension 0, may hold values from 0 to 8191
Outputs:
- born_field: float32 [4, 32, 16, 16, 128], P(('region', 'shot'), 'gz', 'gx'), parts along dimension 0
- factor: float32 [256, 128], P('region'), parts along dimension 0
There are 2 independent parts, one for each index of `region`. A program takes and returns all parts, laid end to end along the dimension named above; each array names one. Nothing has to cross between parts.
All inputs are finite; a program needn't handle non-finite values.
Results may differ from a plain program's by a relative error of at most 0.00013.
Values sent between devices are 32-bit elements; how exact they have to be, the bound alone decides.
A program may use at most 64 MiB of HBM per device.

v0:
```python
import jax
import jax.numpy as jnp
from jax import lax
from jax.sharding import PartitionSpec as P

coefficients = (-205.0 / 72.0, 8.0 / 5.0, -1.0 / 5.0, 8.0 / 315.0, -1.0 / 560.0)
damping = 0.1


def with_halo(cells, sides, width):
    for axis, dim in sides:
        count = lax.axis_size(axis)
        ends = count - 1
        head = lax.slice_in_dim(cells, 0, width, axis=dim)
        tail = lax.slice_in_dim(cells, cells.shape[dim] - width, cells.shape[dim], axis=dim)
        cells = jnp.concatenate(
            [
                lax.ppermute(tail, axis, [(i, (i + 1) % count) for i in range(ends)]),
                cells,
                lax.ppermute(head, axis, [((i + 1) % count, i) for i in range(ends)]),
            ],
            axis=dim,
        )
    return cells


def stencil(padded):
    inner_z = padded.shape[0] - 8
    inner_x = padded.shape[1] - 8
    inner_y = padded.shape[2] - 8

    def window(shift_z, shift_x, shift_y):
        return padded[
            4 + shift_z : 4 + shift_z + inner_z,
            4 + shift_x : 4 + shift_x + inner_x,
            4 + shift_y : 4 + shift_y + inner_y,
        ]

    total = 3.0 * coefficients[0] * window(0, 0, 0)
    for offset in range(1, 5):
        pairs = window(offset, 0, 0) + window(-offset, 0, 0)
        pairs = pairs + window(0, offset, 0) + window(0, -offset, 0)
        pairs = pairs + window(0, 0, offset) + window(0, 0, -offset)
        total = total + coefficients[offset] * pairs
    return total


def square_of(matrix):
    return jnp.dot(
        matrix.T, matrix, precision=lax.Precision.HIGHEST, preferred_element_type=jnp.float32
    )


def local(probes, speed, incident, wavelet, receivers):
    cells_z, cells_x, cells_y, width = probes.shape
    whole_z = cells_z * lax.axis_size("gz")
    whole_x = cells_x * lax.axis_size("gx")
    groups = lax.axis_size("shot")
    steps_count = wavelet.shape[1]
    receiver_count = receivers.shape[1]
    start_z = lax.axis_index("gz") * cells_z
    speed_cells = speed[..., None]
    drive = incident[0][..., None] * probes
    start_x = lax.axis_index("gx") * cells_x
    places = receivers[0]
    global_z = places // (whole_x * cells_y)
    global_x = places // cells_y % whole_x
    global_y = places % cells_y
    local_z = global_z - start_z
    local_x = global_x - start_x
    inside = (local_z >= 0) & (local_z < cells_z) & (local_x >= 0) & (local_x < cells_x)
    local_index = jnp.where(inside, (local_z * cells_x + local_x) * cells_y + global_y, 0)
    weight = inside.astype(jnp.float32)

    def pick(field):
        rows = jnp.take(
            field.reshape(cells_z * cells_x * cells_y, field.shape[3]), local_index, axis=0
        )
        return rows * weight[:, None]

    previous = jnp.zeros_like(drive)
    current = wavelet[0, 0] * drive
    samples = [pick(current)]
    for step in range(1, steps_count):
        padded = with_halo(current, (("gz", 0), ("gx", 1)), 4)
        extended = jnp.pad(padded, ((0, 0), (0, 0), (4, 4), (0, 0)))
        following = (
            2.0 * current - previous + speed_cells * stencil(extended) + wavelet[0, step] * drive
        )
        previous, current = (current, following)
        samples.append(pick(current))
    field = current
    sampled = jnp.concatenate(samples, axis=0)
    flat_probes = probes.reshape(cells_z * cells_x * cells_y, width)
    total_cells = whole_z * whole_x * cells_y
    local_core = square_of(sampled) / (groups * steps_count * receiver_count)
    local_core = local_core + damping / groups * square_of(flat_probes) / total_cells
    whole_core = lax.psum(local_core, ("gz", "shot", "gx"))
    upper = jnp.linalg.cholesky(whole_core).T
    return (field[None], upper)


def solution(mesh):
    placed = (
        P(("region", "gz"), "gx", None, None),
        P(("region", "gz"), "gx", None),
        P(("region", "shot"), "gz", "gx", None),
        P(("region", "shot"), None),
        P(("region", "shot"), None),
    )
    return jax.shard_map(
        local,
        mesh=mesh,
        in_specs=placed,
        out_specs=(P(("region", "shot"), "gz", "gx", None, None), P("region", None)),
        check_vma=False,
    )
```

profile of v0, /device:TPU:0, one launch (start us, length us, event | category | flops | bytes accessed | tf_op | source)
XLA Modules:
  0.0 234.3 jit_solution(5171232568081770694)
XLA Ops:
  8.7 1.8 multiply_multiply_fusion
  11.9 5.6 %collective-permute-start.1 = (f32[4,8,16,128]{3,2,1,0:T(8,128)S(1)}, f32[4,8,16,128]{3,2,1,0:T(8,128)S(1)}, u32[]{:S(2)}, u32[]{:S(2)}) collective-permute-start(f32[4,8,16,128]{3,2,1,0:T(8,128)S(1)} %get-tuple-element.38), channel_id=1, source_target_pairs={{0,4},{4,8},{8,12},{1,5},{5,9},{9,13},{2,6},{6,10},{10,14},{3,7},{... | collective-permute-start | bytes 786440 | tf_op jit(solution)/shard_map/ppermute | solution.py:18
  17.5 4.3 %collective-permute-done = f32[4,8,16,128]{3,2,1,0:T(8,128)S(1)} collective-permute-done((f32[4,8,16,128]{3,2,1,0:T(8,128)S(1)}, f32[4,8,16,128]{3,2,1,0:T(8,128)S(1)}, u32[]{:S(2)}, u32[]{:S(2)}) %collective-permute-start) | collective-permute-done | bytes 262176 | tf_op jit(solution)/shard_map/ppermute | solution.py:20
  26.0 2.3 collective-permute-done.2
  29.9 2.1 fusion.138
  33.4 5.0 %collective-permute-start.5 = (f32[4,8,16,128]{3,2,1,0:T(8,128)S(1)}, f32[4,8,16,128]{3,2,1,0:T(8,128)S(1)}, u32[]{:S(2)}, u32[]{:S(2)}) collective-permute-start(f32[4,8,16,128]{3,2,1,0:T(8,128)S(1)} %get-tuple-element.36), channel_id=1, source_target_pairs={{0,4},{4,8},{8,12},{1,5},{5,9},{9,13},{2,6},{6,10},{10,14},{3,7},{... | collective-permute-start | bytes 786440 | tf_op jit(solution)/shard_map/ppermute | solution.py:18
  38.4 4.7 %collective-permute-done.4 = f32[4,8,16,128]{3,2,1,0:T(8,128)S(1)} collective-permute-done((f32[4,8,16,128]{3,2,1,0:T(8,128)S(1)}, f32[4,8,16,128]{3,2,1,0:T(8,128)S(1)}, u32[]{:S(2)}, u32[]{:S(2)}) %collective-permute-start.4) | collective-permute-done | bytes 262176 | tf_op jit(solution)/shard_map/ppermute | solution.py:20
  47.3 2.3 collective-permute-done.6
  50.4 2.7 %fusion.107 = f32[8,8,16,128]{3,2,1,0:T(8,128)S(1)} fusion(f32[8,8,16,128]{3,2,1,0:T(8,128)S(1)} %fusion.138, f32[4,8,16,128]{3,2,1,0:T(8,128)S(1)} %collective-permute-done.5, f32[4,8,16,128]{3,2,1,0:T(8,128)S(1)} %collective-permute-done.4, f32[16,16,24,128]{3,2,1,0:T(8,128)S(1)} %select_maximum_fusion.12, f32[16,12,16,128]{3,2,1,0:T(8,128)S(1)} %get-tuple-element.22, ...), kind=kLoop, calls=%fused_computation.212 | loop fusion | flops 5898240 | bytes 10493960 | tf_op jit(solution)/shard_map/add | solution.py:88
  54.4 5.0 %collective-permute-start.9 = (f32[4,8,16,128]{3,2,1,0:T(8,128)S(1)}, f32[4,8,16,128]{3,2,1,0:T(8,128)S(1)}, u32[]{:S(2)}, u32[]{:S(2)}) collective-permute-start(f32[4,8,16,128]{3,2,1,0:T(8,128)S(1)} %get-tuple-element.34), channel_id=1, source_target_pairs={{0,4},{4,8},{8,12},{1,5},{5,9},{9,13},{2,6},{6,10},{10,14},{3,7},{... | collective-permute-start | bytes 786440 | tf_op jit(solution)/shard_map/ppermute | solution.py:18
  59.5 4.7 %collective-permute-done.8 = f32[4,8,16,128]{3,2,1,0:T(8,128)S(1)} collective-permute-done((f32[4,8,16,128]{3,2,1,0:T(8,128)S(1)}, f32[4,8,16,128]{3,2,1,0:T(8,128)S(1)}, u32[]{:S(2)}, u32[]{:S(2)}) %collective-permute-start.8) | collective-permute-done | bytes 262176 | tf_op jit(solution)/shard_map/ppermute | solution.py:20
  68.3 2.3 collective-permute-done.10
  71.5 2.1 fusion.76
  75.7 5.0 %collective-permute-start.13 = (f32[4,8,16,128]{3,2,1,0:T(8,128)S(1)}, f32[4,8,16,128]{3,2,1,0:T(8,128)S(1)}, u32[]{:S(2)}, u32[]{:S(2)}) collective-permute-start(f32[4,8,16,128]{3,2,1,0:T(8,128)S(1)} %get-tuple-element.32), channel_id=1, source_target_pairs={{0,4},{4,8},{8,12},{1,5},{5,9},{9,13},{2,6},{6,10},{10,14},{3,7},{... | collective-permute-start | bytes 786440 | tf_op jit(solution)/shard_map/ppermute | solution.py:18
  80.7 4.9 %collective-permute-done.12 = f32[4,8,16,128]{3,2,1,0:T(8,128)S(1)} collective-permute-done((f32[4,8,16,128]{3,2,1,0:T(8,128)}, f32[4,8,16,128]{3,2,1,0:T(8,128)S(1)}, u32[]{:S(2)}, u32[]{:S(2)}) %collective-permute-start.12) | collective-permute-done | bytes 262176 | tf_op jit(solution)/shard_map/ppermute | solution.py:20
  87.7 2.1 collective-permute-start.15
  91.7 2.2 collective-permute-done.14
  93.9 1.7 select_maximum_fusion.4
  97.1 2.1 fusion.45
  101.3 5.0 %collective-permute-start.17 = (f32[4,8,16,128]{3,2,1,0:T(8,128)}, f32[4,8,16,128]{3,2,1,0:T(8,128)S(1)}, u32[]{:S(2)}, u32[]{:S(2)}) collective-permute-start(f32[4,8,16,128]{3,2,1,0:T(8,128)} %get-tuple-element.30), channel_id=1, source_target_pairs={{0,4},{4,8},{8,12},{1,5},{5,9},{9,13},{2,6},{6,10},{10,14},{3,7},{... | collective-permute-start | bytes 786440 | tf_op jit(solution)/shard_map/ppermute | solution.py:18
  107.7 3.5 %collective-permute-done.16 = f32[4,8,16,128]{3,2,1,0:T(8,128)S(1)} collective-permute-done((f32[4,8,16,128]{3,2,1,0:T(8,128)}, f32[4,8,16,128]{3,2,1,0:T(8,128)S(1)}, u32[]{:S(2)}, u32[]{:S(2)}) %collective-permute-start.16) | collective-permute-done | bytes 262176 | tf_op jit(solution)/shard_map/ppermute | solution.py:20
  119.8 2.1 fusion.14
  124.7 87.2 %all-reduce.7.cloned.1.call-done = f32[128,128]{0,1:T(8,128)} async-done(((f32[128,128]{0,1:T(8,128)}), f32[128,128]{0,1:T(8,128)}) %all-reduce.7.cloned.1.call-update) | async-done | bytes 65552 | tf_op jit(solution)/shard_map/psum | solution.py:98
  213.7 11.7 %cholesky.18 = f32[128,128]{1,0:T(8,128)S(1)} custom-call(f32[128,128]{1,0:T(8,128)S(1)} %fusion.168), custom_call_target="Cholesky" | custom-call | tf_op jit(solution)/shard_map/jit(cholesky)/cholesky | solution.py:99
  (85 shorter events, 47.4 us)
Async XLA Ops:
  7.2 204.8 %all-reduce.7.cloned.1.call-start = ((), (), s32[]{:S(2)}) async-start(), calls=%async_computation | async-start | bytes 131072 | tf_op jit(solution)/shard_map/psum | solution.py:98
  10.6 11.2 %collective-permute-start = (f32[4,8,16,128]{3,2,1,0:T(8,128)S(1)}, f32[4,8,16,128]{3,2,1,0:T(8,128)S(1)}, u32[]{:S(2)}, u32[]{:S(2)}) collective-permute-start(f32[4,8,16,128]{3,2,1,0:T(8,128)S(1)} %get-tuple-element.37), channel_id=1, source_target_pairs={{4,0},{8,4},{12,8},{5,1},{9,5},{13,9},{6,2},{10,6},{14,10},{7,3},{... | collective-permute-start | bytes 786440 | tf_op jit(solution)/shard_map/ppermute | solution.py:20
  11.9 11.1 %collective-permute-start.1 = (f32[4,8,16,128]{3,2,1,0:T(8,128)S(1)}, f32[4,8,16,128]{3,2,1,0:T(8,128)S(1)}, u32[]{:S(2)}, u32[]{:S(2)}) collective-permute-start(f32[4,8,16,128]{3,2,1,0:T(8,128)S(1)} %get-tuple-element.38), channel_id=1, source_target_pairs={{0,4},{4,8},{8,12},{1,5},{5,9},{9,13},{2,6},{6,10},{10,14},{3,7},{... | collective-permute-start | bytes 786440 | tf_op jit(solution)/shard_map/ppermute | solution.py:18
  23.2 2.8 %collective-permute-start.3 = (f32[16,4,16,128]{3,2,1,0:T(8,128)S(1)}, f32[16,4,16,128]{3,2,1,0:T(8,128)S(1)}, u32[]{:S(2)}, u32[]{:S(2)}) collective-permute-start(f32[16,4,16,128]{3,2,1,0:T(8,128)S(1)} %get-tuple-element.27), channel_id=1, source_target_pairs={{0,1},{2,3},{4,5},{6,7},{8,9},{10,11},{12,13},{14,15},{16,17},{18,... | collective-permute-start | bytes 1572872 | tf_op jit(solution)/shard_map/ppermute | solution.py:18
  24.5 3.8 %collective-permute-start.2 = (f32[16,4,16,128]{3,2,1,0:T(8,128)S(1)}, f32[16,4,16,128]{3,2,1,0:T(8,128)S(1)}, u32[]{:S(2)}, u32[]{:S(2)}) collective-permute-start(f32[16,4,16,128]{3,2,1,0:T(8,128)S(1)} %get-tuple-element.28), channel_id=1, source_target_pairs={{1,0},{3,2},{5,4},{7,6},{9,8},{11,10},{13,12},{15,14},{17,16},{19,... | collective-permute-start | bytes 1572872 | tf_op jit(solution)/shard_map/ppermute | solution.py:20
  28.9 1.0 copy-start
  32.1 11.0 %collective-permute-start.4 = (f32[4,8,16,128]{3,2,1,0:T(8,128)S(1)}, f32[4,8,16,128]{3,2,1,0:T(8,128)S(1)}, u32[]{:S(2)}, u32[]{:S(2)}) collective-permute-start(f32[4,8,16,128]{3,2,1,0:T(8,128)S(1)} %get-tuple-element.35), channel_id=1, source_target_pairs={{4,0},{8,4},{12,8},{5,1},{9,5},{13,9},{6,2},{10,6},{14,10},{7,3},{... | collective-permute-start | bytes 786440 | tf_op jit(solution)/shard_map/ppermute | solution.py:20
  33.4 10.9 %collective-permute-start.5 = (f32[4,8,16,128]{3,2,1,0:T(8,128)S(1)}, f32[4,8,16,128]{3,2,1,0:T(8,128)S(1)}, u32[]{:S(2)}, u32[]{:S(2)}) collective-permute-start(f32[4,8,16,128]{3,2,1,0:T(8,128)S(1)} %get-tuple-element.36), channel_id=1, source_target_pairs={{0,4},{4,8},{8,12},{1,5},{5,9},{9,13},{2,6},{6,10},{10,14},{3,7},{... | collective-permute-start | bytes 786440 | tf_op jit(solution)/shard_map/ppermute | solution.py:18
  44.4 2.8 %collective-permute-start.7 = (f32[16,4,16,128]{3,2,1,0:T(8,128)S(1)}, f32[16,4,16,128]{3,2,1,0:T(8,128)S(1)}, u32[]{:S(2)}, u32[]{:S(2)}) collective-permute-start(f32[16,4,16,128]{3,2,1,0:T(8,128)S(1)} %get-tuple-element.23), channel_id=1, source_target_pairs={{0,1},{2,3},{4,5},{6,7},{8,9},{10,11},{12,13},{14,15},{16,17},{18,... | collective-permute-start | bytes 1572872 | tf_op jit(solution)/shard_map/ppermute | solution.py:18
  45.8 3.8 %collective-permute-start.6 = (f32[16,4,16,128]{3,2,1,0:T(8,128)S(1)}, f32[16,4,16,128]{3,2,1,0:T(8,128)S(1)}, u32[]{:S(2)}, u32[]{:S(2)}) collective-permute-start(f32[16,4,16,128]{3,2,1,0:T(8,128)S(1)} %get-tuple-element.24), channel_id=1, source_target_pairs={{1,0},{3,2},{5,4},{7,6},{9,8},{11,10},{13,12},{15,14},{17,16},{19,... | collective-permute-start | bytes 1572872 | tf_op jit(solution)/shard_map/ppermute | solution.py:20
  53.1 11.0 %collective-permute-start.8 = (f32[4,8,16,128]{3,2,1,0:T(8,128)S(1)}, f32[4,8,16,128]{3,2,1,0:T(8,128)S(1)}, u32[]{:S(2)}, u32[]{:S(2)}) collective-permute-start(f32[4,8,16,128]{3,2,1,0:T(8,128)S(1)} %get-tuple-element.33), channel_id=1, source_target_pairs={{4,0},{8,4},{12,8},{5,1},{9,5},{13,9},{6,2},{10,6},{14,10},{7,3},{... | collective-permute-start | bytes 786440 | tf_op jit(solution)/shard_map/ppermute | solution.py:20
  54.4 10.9 %collective-permute-start.9 = (f32[4,8,16,128]{3,2,1,0:T(8,128)S(1)}, f32[4,8,16,128]{3,2,1,0:T(8,128)S(1)}, u32[]{:S(2)}, u32[]{:S(2)}) collective-permute-start(f32[4,8,16,128]{3,2,1,0:T(8,128)S(1)} %get-tuple-element.34), channel_id=1, source_target_pairs={{0,4},{4,8},{8,12},{1,5},{5,9},{9,13},{2,6},{6,10},{10,14},{3,7},{... | collective-permute-start | bytes 786440 | tf_op jit(solution)/shard_map/ppermute | solution.py:18
  65.5 2.8 %collective-permute-start.11 = (f32[16,4,16,128]{3,2,1,0:T(8,128)S(1)}, f32[16,4,16,128]{3,2,1,0:T(8,128)S(1)}, u32[]{:S(2)}, u32[]{:S(2)}) collective-permute-start(f32[16,4,16,128]{3,2,1,0:T(8,128)S(1)} %get-tuple-element.19), channel_id=1, source_target_pairs={{0,1},{2,3},{4,5},{6,7},{8,9},{10,11},{12,13},{14,15},{16,17},{18,... | collective-permute-start | bytes 1572872 | tf_op jit(solution)/shard_map/ppermute | solution.py:18
  66.8 3.8 %collective-permute-start.10 = (f32[16,4,16,128]{3,2,1,0:T(8,128)S(1)}, f32[16,4,16,128]{3,2,1,0:T(8,128)S(1)}, u32[]{:S(2)}, u32[]{:S(2)}) collective-permute-start(f32[16,4,16,128]{3,2,1,0:T(8,128)S(1)} %get-tuple-element.20), channel_id=1, source_target_pairs={{1,0},{3,2},{5,4},{7,6},{9,8},{11,10},{13,12},{15,14},{17,16},{19,... | collective-permute-start | bytes 1572872 | tf_op jit(solution)/shard_map/ppermute | solution.py:20
  73.6 17.4 %copy-start.4 = (s32[1,64]{1,0:T(1,128)S(1)}, s32[1,64]{1,0:T(1,128)}, u32[]{:S(2)}) copy-start(s32[1,64]{1,0:T(1,128)} %param.11) | copy-start | bytes 772
  74.4 11.2 %collective-permute-start.12 = (f32[4,8,16,128]{3,2,1,0:T(8,128)}, f32[4,8,16,128]{3,2,1,0:T(8,128)S(1)}, u32[]{:S(2)}, u32[]{:S(2)}) collective-permute-start(f32[4,8,16,128]{3,2,1,0:T(8,128)} %get-tuple-element.31), channel_id=1, source_target_pairs={{4,0},{8,4},{12,8},{5,1},{9,5},{13,9},{6,2},{10,6},{14,10},{7,3},{... | collective-permute-start | bytes 786440 | tf_op jit(solution)/shard_map/ppermute | solution.py:20
  75.7 10.9 %collective-permute-start.13 = (f32[4,8,16,128]{3,2,1,0:T(8,128)S(1)}, f32[4,8,16,128]{3,2,1,0:T(8,128)S(1)}, u32[]{:S(2)}, u32[]{:S(2)}) collective-permute-start(f32[4,8,16,128]{3,2,1,0:T(8,128)S(1)} %get-tuple-element.32), channel_id=1, source_target_pairs={{0,4},{4,8},{8,12},{1,5},{5,9},{9,13},{2,6},{6,10},{10,14},{3,7},{... | collective-permute-start | bytes 786440 | tf_op jit(solution)/shard_map/ppermute | solution.py:18
  87.7 4.0 %collective-permute-start.15 = (f32[16,4,16,128]{3,2,1,0:T(8,128)}, f32[16,4,16,128]{3,2,1,0:T(8,128)}, u32[]{:S(2)}, u32[]{:S(2)}) collective-permute-start(f32[16,4,16,128]{3,2,1,0:T(8,128)} %get-tuple-element.15), channel_id=1, source_target_pairs={{0,1},{2,3},{4,5},{6,7},{8,9},{10,11},{12,13},{14,15},{16,17},{18,... | collective-permute-start | bytes 1572872 | tf_op jit(solution)/shard_map/ppermute | solution.py:18
  89.7 4.1 %collective-permute-start.14 = (f32[16,4,16,128]{3,2,1,0:T(8,128)}, f32[16,4,16,128]{3,2,1,0:T(8,128)}, u32[]{:S(2)}, u32[]{:S(2)}) collective-permute-start(f32[16,4,16,128]{3,2,1,0:T(8,128)} %get-tuple-element.16), channel_id=1, source_target_pairs={{1,0},{3,2},{5,4},{7,6},{9,8},{11,10},{13,12},{15,14},{17,16},{19,... | collective-permute-start | bytes 1572872 | tf_op jit(solution)/shard_map/ppermute | solution.py:20
  100.0 11.2 %collective-permute-start.16 = (f32[4,8,16,128]{3,2,1,0:T(8,128)}, f32[4,8,16,128]{3,2,1,0:T(8,128)S(1)}, u32[]{:S(2)}, u32[]{:S(2)}) collective-permute-start(f32[4,8,16,128]{3,2,1,0:T(8,128)} %get-tuple-element.29), channel_id=1, source_target_pairs={{4,0},{8,4},{12,8},{5,1},{9,5},{13,9},{6,2},{10,6},{14,10},{7,3},{... | collective-permute-start | bytes 786440 | tf_op jit(solution)/shard_map/ppermute | solution.py:20
  101.3 11.2 %collective-permute-start.17 = (f32[4,8,16,128]{3,2,1,0:T(8,128)}, f32[4,8,16,128]{3,2,1,0:T(8,128)S(1)}, u32[]{:S(2)}, u32[]{:S(2)}) collective-permute-start(f32[4,8,16,128]{3,2,1,0:T(8,128)} %get-tuple-element.30), channel_id=1, source_target_pairs={{0,4},{4,8},{8,12},{1,5},{5,9},{9,13},{2,6},{6,10},{10,14},{3,7},{... | collective-permute-start | bytes 786440 | tf_op jit(solution)/shard_map/ppermute | solution.py:18
  113.6 4.3 %collective-permute-start.19 = (f32[16,4,16,128]{3,2,1,0:T(8,128)}, f32[16,4,16,128]{3,2,1,0:T(8,128)S(1)}, u32[]{:S(2)}, u32[]{:S(2)}) collective-permute-start(f32[16,4,16,128]{3,2,1,0:T(8,128)} %get-tuple-element.11), channel_id=1, source_target_pairs={{0,1},{2,3},{4,5},{6,7},{8,9},{10,11},{12,13},{14,15},{16,17},{18,... | collective-permute-start | bytes 1572872 | tf_op jit(solution)/shard_map/ppermute | solution.py:18
  115.0 4.0 %collective-permute-start.18 = (f32[16,4,16,128]{3,2,1,0:T(8,128)}, f32[16,4,16,128]{3,2,1,0:T(8,128)S(1)}, u32[]{:S(2)}, u32[]{:S(2)}) collective-permute-start(f32[16,4,16,128]{3,2,1,0:T(8,128)} %get-tuple-element.12), channel_id=1, source_target_pairs={{1,0},{3,2},{5,4},{7,6},{9,8},{11,10},{13,12},{15,14},{17,16},{19,... | collective-permute-start | bytes 1572872 | tf_op jit(solution)/shard_map/ppermute | solution.py:20
  121.9 105.6 %copy-start.2 = (f32[8,8,16,128]{3,2,1,0:T(8,128)}, f32[8,8,16,128]{3,2,1,0:T(8,128)S(1)}, u32[]{:S(2)}) copy-start(f32[8,8,16,128]{3,2,1,0:T(8,128)S(1)} %fusion.14) | copy-start | bytes 1572868
  (2 other events, 2.1 us)
Sparse Core Ops, SparseCore 0:
  124.9 87.0 all-reduce.6
where the time goes:
time: 236 us; the launch traced here: 234 us
  waiting for transfers between devices  126 us (53%)
  starting transfers between devices  46.1 us (20%)
  other arithmetic  34.2 us (14%)
  between operations  14.6 us (6%)
  local copies, waits for them, and re-layouts  11.6 us (5%)
    psum x1, waiting for transfers between devices, local(): whole_core = lax.psum(local_core, ('gz', 'shot', 'gx'))  87.2 us
    ppermute x10, starting transfers between devices, with_halo(): lax.ppermute(tail, axis, [(i, (i + 1) % count) for i in range(ends)])  33 us
    ppermute x10, waiting for transfers between devices, with_halo(): lax.ppermute(head, axis, [((i + 1) % count, i) for i in range(ends)])  32.2 us
    ppermute x10, starting transfers between devices, with_halo(): lax.ppermute(head, axis, [((i + 1) % count, i) for i in range(ends)])  13.1 us
    another operation x3, other arithmetic, local(): upper = jnp.linalg.cholesky(whole_core).T  12.4 us
    add x5, other arithmetic, local(): 2.0 * current - previous + speed_cells * stencil(extended)  11.1 us
    concatenate x15, other arithmetic, with_halo(): jnp.concatenate([lax.ppermute(tail, axis, [(i, (i + 1) % count) for i in...  6.94 us
    ppermute x10, waiting for transfers between devices, with_halo(): lax.ppermute(tail, axis, [(i, (i + 1) % count) for i in range(ends)])  6.36 us
  transfers between devices with their start and end apart: 21, of which 19 were waited for; matrix products, arithmetic and copies ran while one was open for 1% of the time, Pallas kernels for 0%

commit v1 on v0

v1 whole, which is shorter than its diff:
```python
import functools

import jax
import jax.numpy as jnp
from jax import lax
from jax.experimental import pallas as pl
from jax.experimental.pallas import tpu as pltpu
from jax.sharding import PartitionSpec as P

coefficients = (-205.0 / 72.0, 8.0 / 5.0, -1.0 / 5.0, 8.0 / 315.0, -1.0 / 560.0)
damping = 0.1
HIGH = lax.Precision.HIGHEST
F32 = jnp.float32
PAD = 8
DEPTH = 4


def gram_of(rows):
    return lax.dot_general(
        rows, rows, (((0,), (0,)), ((), ())), precision=HIGH, preferred_element_type=F32
    )


def kernel(
    sizes,
    wavelet,
    rows_at,
    probes,
    medium,
    group_of,
    out,
    factor,
    fields,
    flat,
    drive,
    speed,
    send,
    recv,
    media,
    picked,
    out_a,
    in_a,
    all_a,
    out_b,
    in_b,
    all_b,
    core,
    pack_s,
    pack_r,
    med_s,
    med_r,
    x_s,
    x_r,
    a_s,
    a_r,
    ba_s,
    ba_r,
    b_s,
    b_r,
    bb_s,
    bb_r,
    o_s,
    o_r,
):
    nz, ns, cz, cx, cy, width, steps, receivers = sizes
    cells = cz * cx
    part = cells // nz
    group = width // nz
    members = nz * 2
    everyone = members * ns
    owners = min(members, receivers // 8)
    own_rows = receivers // owners
    gram_rows = width // owners
    early = (steps - 1) * own_rows

    z = lax.axis_index("gz")
    s = lax.axis_index("shot")
    x = lax.axis_index("gx")
    m = z * 2 + x
    f = s * members + m
    lanes = lax.broadcasted_iota(jnp.int32, (cy, width), 1) // group

    def remote(src, dst, ss, rs, tz, ts, tx):
        return pltpu.make_async_remote_copy(
            src_ref=src,
            dst_ref=dst,
            send_sem=ss,
            recv_sem=rs,
            device_id={"gz": tz, "shot": ts, "gx": tx},
            device_id_type=pl.DeviceIdType.MESH,
        )

    def split(t):
        ts = t // members
        tm = t % members
        return ts, tm, tm // 2, tm % 2

    barrier = pltpu.get_barrier_semaphore()

    def greet(i, c):
        ts, _, tz, tx = split((f + 1 + i) % everyone)
        pl.semaphore_signal(
            barrier,
            inc=1,
            device_id={"gz": tz, "shot": ts, "gx": tx},
            device_id_type=pl.DeviceIdType.MESH,
        )
        return c

    lax.fori_loop(0, everyone - 1, greet, 0)

    def pack(source, zd):
        def body(c, carry):
            acc = None
            for q in range(nz):
                part_q = source(q * part + c)
                shift = (group * (q - zd)) % width
                if shift:
                    part_q = pltpu.roll(part_q, shift, 1)
                acc = part_q if acc is None else jnp.where(lanes == q, part_q, acc)
            send[zd, c] = acc
            return carry

        lax.fori_loop(0, part, body, 0, unroll=2)

    def unpack(target):
        for q in range(nz):

            def body(c, carry):
                acc = None
                for zs in range(nz):
                    piece = recv[zs, c]
                    shift = (group * (zs - q)) % width
                    if shift:
                        piece = pltpu.roll(piece, shift, 1)
                    acc = piece if acc is None else jnp.where(lanes == zs, piece, acc)
                target(q * part + c, acc)
                return carry

            lax.fori_loop(0, part, body, 0, unroll=2)

    for zd in range(nz):
        pack(lambda i: probes[i], zd)
    pl.semaphore_wait(barrier, everyone - 1)

    def exchange_start(ss, rs, land):
        def body(i, c):
            tz = (z + 1 + i) % nz
            remote(send.at[tz], land.at[z], ss.at[tz], rs.at[z], tz, s, x).start()
            return c

        lax.fori_loop(0, nz - 1, body, 0)

    def exchange_wait(ss, rs, land):
        def body(i, c):
            tz = (z + 1 + i) % nz
            remote(send.at[tz], land.at[tz], ss.at[tz], rs.at[tz], tz, s, x).wait()
            return c

        lax.fori_loop(0, nz - 1, body, 0)

    def media_body(wait):
        def body(i, c):
            tz = (z + 1 + i) % nz
            here = media.at[tz] if wait else media.at[z]
            copy = remote(
                medium, here, med_s.at[tz], med_r.at[tz if wait else z], tz, s, x
            )
            if wait:
                copy.wait()
            else:
                copy.start()
            return c

        lax.fori_loop(0, nz - 1, body, 0)

    media_body(False)
    exchange_start(pack_s, pack_r, recv)
    media[z] = medium[...]
    recv[z] = send[z]

    zeros = jnp.zeros((PAD, width), F32)
    blank = jnp.zeros((cy, width), F32)
    outer = (cx + DEPTH) * x
    for n in range(steps - 1):

        def clear(i, c):
            for j in range(cx):
                fields[n, DEPTH + i, DEPTH + j, 0:PAD] = zeros
                fields[n, DEPTH + i, DEPTH + j, PAD + cy : PAD + cy + PAD] = zeros
            for j in range(DEPTH):
                fields[n, DEPTH + i, outer + j, PAD : PAD + cy] = blank
            return c

        lax.fori_loop(0, cz, clear, 0)

    probe_gram = gram_of(probes[...].reshape(cells * cy, width))
    for o in range(owners):
        out_a[o, early : early + gram_rows] = probe_gram[o * gram_rows : (o + 1) * gram_rows]

    media_body(True)
    columns = cx * cy
    zrow = lax.broadcasted_iota(jnp.int32, (nz * cz, width), 0)
    zlane = lax.broadcasted_iota(jnp.int32, (nz * cz, width), 1) // group
    spread_speed = media[:, 0].reshape(nz * cz, columns)
    spread_incident = media[:, 1].reshape(nz * cz, columns)
    for i in range(cz):
        onehot = (zrow == zlane * cz + i).astype(F32)
        for spread, target in ((spread_speed, speed), (spread_incident, drive)):
            target[i * cx : (i + 1) * cx] = lax.dot_general(
                spread, onehot, (((0,), (0,)), ((), ())), precision=HIGH, preferred_element_type=F32
            ).reshape(cx, cy, width)

    exchange_wait(pack_s, pack_r, recv)

    def set_drive(i, value):
        drive[i] = drive[i] * value

    unpack(set_drive)

    low = lanes == 0
    high = lanes == nz - 1

    def put(n, i, j, value):
        flat[pl.ds((i * cx + j) * cy, cy)] = value
        if n < steps - 1:
            fields[n, DEPTH + i, DEPTH + j, PAD : PAD + cy] = value

    def fold(n):
        for i in range(DEPTH):

            def body(j, c):
                rows = pl.ds(PAD, cy)
                below = fields[n, DEPTH + cz - DEPTH + i, DEPTH + j, rows]
                above = fields[n, DEPTH + i, DEPTH + j, rows]
                below = jnp.where(low, 0.0, pltpu.roll(below, group, 1))
                above = jnp.where(high, 0.0, pltpu.roll(above, width - group, 1))
                fields[n, i, DEPTH + j, rows] = below
                fields[n, DEPTH + cz + i, DEPTH + j, rows] = above
                return c

            lax.fori_loop(0, cx, body, 0, unroll=2)

    near = (cx - DEPTH) * (1 - x)
    far = (cx - DEPTH) - near

    def border(n, wait):
        src = fields.at[n, pl.ds(DEPTH, cz), pl.ds(DEPTH + near, DEPTH), pl.ds(PAD, cy)]
        at = (cx + DEPTH) * (1 - x) if wait else (cx + DEPTH) * x
        dst = fields.at[n, pl.ds(DEPTH, cz), pl.ds(at, DEPTH), pl.ds(PAD, cy)]
        return remote(src, dst, x_s.at[n], x_r.at[n], z, s, 1 - x)

    def advance(n, start):
        amplitude = wavelet[0, n]

        def body(i, c):
            for jj in range(DEPTH):
                j = start + jj
                a, b = DEPTH + i, DEPTH + j
                now = fields[n - 1, a, b, PAD : PAD + cy]
                total = (3.0 * coefficients[0]) * now
                for k in range(1, DEPTH + 1):
                    pairs = fields[n - 1, a + k, b, PAD : PAD + cy] + fields[n - 1, a - k, b, PAD : PAD + cy]
                    pairs += fields[n - 1, a, b + k, PAD : PAD + cy] + fields[n - 1, a, b - k, PAD : PAD + cy]
                    pairs += fields[n - 1, a, b, PAD + k : PAD + k + cy] + fields[n - 1, a, b, PAD - k : PAD - k + cy]
                    total += coefficients[k] * pairs
                cell = i * cx + j
                value = 2.0 * now + speed[cell] * total + amplitude * drive[cell]
                if n > 1:
                    value -= fields[n - 2, a, b, PAD : PAD + cy]
                put(n, i, j, value)
            return c

        lax.fori_loop(0, cz, body, 0)

    wide = lax.broadcasted_iota(jnp.int32, (receivers, width), 1) // group

    def pick(n):
        for r in range(receivers):
            picked[r : r + 1] = flat[pl.ds(rows_at[0, r], 1)]
        rows = jnp.where(wide == group_of[...], picked[...], 0.0)
        shift = group
        while shift < width:
            rows = rows + pltpu.roll(rows, shift, 1)
            shift *= 2
        rows = jnp.where(wide == z, rows, 0.0)
        for o in range(owners):
            piece = rows[o * own_rows : (o + 1) * own_rows]
            if n < steps - 1:
                out_a[o, n * own_rows : (n + 1) * own_rows] = piece
            else:
                out_b[o] = piece

    def only(condition, body):
        if owners == members:
            body()
        else:
            pl.when(condition)(body)

    def to_owners(outgoing, incoming, ss, rs, act):
        def body(i, c):
            t = (m + 1 + i) % members

            def start():
                remote(
                    outgoing.at[t], incoming.at[m], ss.at[t], rs.at[m], t // 2, s, t % 2
                ).start()

            def sent():
                remote(
                    outgoing.at[t], incoming.at[m], ss.at[t], rs.at[m], t // 2, s, t % 2
                ).wait_send()

            def arrived():
                remote(
                    outgoing.at[0], incoming.at[t], ss.at[t], rs.at[t], t // 2, s, t % 2
                ).wait_recv()

            if act == "arrived":
                only(m < owners, arrived)
            else:
                only(t < owners, start if act == "start" else sent)
            return c

        lax.fori_loop(0, members - 1, body, 0)

    def sum_up(outgoing, incoming, spread):
        def body():
            incoming[m] = outgoing[m]
            total = incoming[0]
            for t in range(1, members):
                total = total + incoming[t]
            spread[s, m] = total

        only(m < owners, body)

    def to_all(spread, ss, rs, act):
        def body(i, c):
            t = (f + 1 + i) % everyone
            ts, tm, tz, tx = split(t)

            def start():
                remote(spread.at[s, m], spread.at[s, m], ss.at[t], rs.at[f], tz, ts, tx).start()

            def sent():
                remote(spread.at[s, m], spread.at[s, m], ss.at[t], rs.at[f], tz, ts, tx).wait_send()

            def arrived():
                remote(spread.at[ts, tm], spread.at[ts, tm], ss.at[t], rs.at[t], tz, ts, tx).wait_recv()

            if act == "arrived":
                only(tm < owners, arrived)
            else:
                only(m < owners, start if act == "start" else sent)
            return c

        lax.fori_loop(0, everyone - 1, body, 0)

    first = wavelet[0, 0]

    def begin(i, c):
        for j in range(cx):
            put(0, i, j, first * drive[i * cx + j])
        return c

    lax.fori_loop(0, cz, begin, 0)
    border(0, False).start()
    fold(0)
    pick(0)
    for n in range(1, steps):
        advance(n, far)
        if n == steps - 1:
            to_owners(out_a, in_a, a_s, a_r, "arrived")
            sum_up(out_a, in_a, all_a)
            to_all(all_a, ba_s, ba_r, "start")
        border(n - 1, True).wait_recv()
        advance(n, near)
        if n < steps - 1:
            border(n, False).start()
            fold(n)
        pick(n)
        if n == steps - 2:
            to_owners(out_a, in_a, a_s, a_r, "start")
    to_owners(out_b, in_b, b_s, b_r, "start")
    for zd in range(nz):
        pack(lambda i: flat[pl.ds(pl.multiple_of(i * cy, cy), cy)], zd)
    to_owners(out_b, in_b, b_s, b_r, "arrived")
    sum_up(out_b, in_b, all_b)
    to_all(all_b, bb_s, bb_r, "start")

    to_all(all_a, ba_s, ba_r, "arrived")
    sampled = all_a[:, :, 0:early].reshape(ns * owners * early, width)
    probe_part = jnp.zeros((width, width), F32)
    probe_part = all_a[s, :, early : early + gram_rows].reshape(width, width)
    total_cells = float(nz * cz * 2 * cx * cy)
    count = float(ns * steps * receivers)
    core[...] = gram_of(sampled) / count + damping * probe_part / total_cells
    to_all(all_b, bb_s, bb_r, "arrived")
    exchange_start(o_s, o_r, recv)
    recv[z] = send[z]
    core[...] += gram_of(all_b[...].reshape(ns * owners * own_rows, width)) / count

    panel = 8
    row_in = lax.broadcasted_iota(jnp.int32, (panel, width), 0)
    col_in = lax.broadcasted_iota(jnp.int32, (panel, width), 1)
    for p in range(width // panel):
        top = p * panel
        block = core[top : top + panel]
        diag = [
            jnp.broadcast_to(block[:, top + k : top + k + 1], (panel, width)) for k in range(panel)
        ]
        for k in range(panel):
            scale = lax.rsqrt(jnp.broadcast_to(diag[k][k : k + 1], (panel, width)))
            pivot = jnp.broadcast_to(block[k : k + 1], (panel, width)) * scale
            below = jnp.where(row_in > k, diag[k] * scale, 0.0)
            block = jnp.where(row_in == k, pivot, block - below * pivot)
            for l in range(k + 1, panel):
                side = jnp.broadcast_to(diag[l][k : k + 1], (panel, width)) * scale
                diag[l] = diag[l] - below * side
        block = jnp.where(col_in >= row_in + top, block, 0.0)
        factor[top : top + panel] = block
        if top + panel < width:
            rest = lax.dot_general(
                block,
                block,
                (((0,), (0,)), ((), ())),
                precision=HIGH,
                preferred_element_type=F32,
            )
            core[top + panel :] -= rest[top + panel :]

    exchange_wait(o_s, o_r, recv)

    def set_out(i, value):
        out[i] = value

    unpack(set_out)

    for n in range(steps - 1):
        border(n, False).wait_send()
    to_owners(out_a, in_a, a_s, a_r, "sent")
    to_owners(out_b, in_b, b_s, b_r, "sent")
    to_all(all_a, ba_s, ba_r, "sent")
    to_all(all_b, bb_s, bb_r, "sent")


def local(probes, speed, incident, wavelet, receivers):
    cz, cx, cy, width = probes.shape
    nz = lax.axis_size("gz")
    nx = lax.axis_size("gx")
    ns = lax.axis_size("shot")
    steps = wavelet.shape[1]
    count = receivers.shape[1]
    places = receivers[0]
    whole_x = cx * nx
    at_z = places // (whole_x * cy)
    at_x = places // cy % whole_x
    at_y = places % cy
    rows_at = ((at_z % cz * cx + at_x % cx) * cy + at_y)[None]
    inside = at_x // cx == lax.axis_index("gx")
    group_of = jnp.where(inside, at_z // cz, -1)[:, None]
    medium = jnp.stack([speed.reshape(cz, cx * cy), incident[0].reshape(cz, cx * cy)])
    cells = cz * cx
    members = nz * nx
    everyone = members * ns
    owners = min(members, count // 8)
    own_rows = count // owners
    message = (steps - 1) * own_rows + width // owners
    part = cells // nz
    dma = pltpu.SemaphoreType.DMA
    vmem = pl.BlockSpec(memory_space=pltpu.VMEM)
    smem = pl.BlockSpec(memory_space=pltpu.SMEM)
    sizes = (nz, ns, cz, cx, cy, width, steps, count)
    field, factor = pl.pallas_call(
        functools.partial(kernel, sizes),
        out_shape=(
            jax.ShapeDtypeStruct((cells, cy, width), F32),
            jax.ShapeDtypeStruct((width, width), F32),
        ),
        in_specs=[smem, smem, vmem, vmem, vmem],
        out_specs=(vmem, vmem),
        scratch_shapes=[
            pltpu.VMEM((steps - 1, cz + 2 * DEPTH, cx + 2 * DEPTH, cy + 2 * PAD, width), F32),
            pltpu.VMEM((cells * cy, width), F32),
            pltpu.VMEM((cells, cy, width), F32),
            pltpu.VMEM((cells, cy, width), F32),
            pltpu.VMEM((nz, part, cy, width), F32),
            pltpu.VMEM((nz, part, cy, width), F32),
            pltpu.VMEM((nz, 2, cz, cx * cy), F32),
            pltpu.VMEM((count, width), F32),
            pltpu.VMEM((owners, message, width), F32),
            pltpu.VMEM((members, message, width), F32),
            pltpu.VMEM((ns, owners, message, width), F32),
            pltpu.VMEM((owners, own_rows, width), F32),
            pltpu.VMEM((members, own_rows, width), F32),
            pltpu.VMEM((ns, owners, own_rows, width), F32),
            pltpu.VMEM((width, width), F32),
            dma((nz,)),
            dma((nz,)),
            dma((nz,)),
            dma((nz,)),
            dma((steps - 1,)),
            dma((steps - 1,)),
            dma((members,)),
            dma((members,)),
            dma((everyone,)),
            dma((everyone,)),
            dma((members,)),
            dma((members,)),
            dma((everyone,)),
            dma((everyone,)),
            dma((nz,)),
            dma((nz,)),
        ],
        compiler_params=pltpu.CompilerParams(
            collective_id=0, has_side_effects=True, vmem_limit_bytes=48 * 1024 * 1024
        ),
    )(wavelet, rows_at, probes.reshape(cells, cy, width), medium, group_of)
    return (field.reshape(1, cz, cx, cy, width), factor)


def solution(mesh):
    placed = (
        P(("region", "gz"), "gx", None, None),
        P(("region", "gz"), "gx", None),
        P(("region", "shot"), "gz", "gx", None),
        P(("region", "shot"), None),
        P(("region", "shot"), None),
    )
    return jax.shard_map(
        local,
        mesh=mesh,
        in_specs=placed,
        out_specs=(P(("region", "shot"), "gz", "gx", None, None), P("region", None)),
        check_vma=False,
    )
```

time: 236 us -> 78.9 us (0.33)
  waiting for transfers between devices: 126 us -> 0 us
  Pallas kernels: 0 us -> 72.5 us
  starting transfers between devices: 46.1 us -> 0 us
  other arithmetic: 34.2 us -> 0.78 us
  between operations: 14.6 us -> 0.66 us
  local copies, waits for them, and re-layouts: 11.6 us -> 4.68 us
    psum x1 -> x0, waiting for transfers between devices: 87.2 us -> none  [local(): whole_core = lax.psum(local_core, ('gz', 'shot', 'gx'))]
    pallas_call x0 -> x1, Pallas kernels: none -> 72.5 us  [local(): pl.pallas_call(functools.partial(kernel, sizes), out_shape=(jax.ShapeDtyp...]
    ppermute x20 -> x0, starting transfers between devices: 46.1 us -> none  [the longest x10 33 us: with_halo(): lax.ppermute(tail, axis, [(i, (i + 1) % count) for i in range(ends)])]
    ppermute x20 -> x0, waiting for transfers between devices: 38.5 us -> none  [the longest x10 32.2 us: with_halo(): lax.ppermute(head, axis, [((i + 1) % count, i) for i in range(ends)])]
    another operation x3 -> x1, other arithmetic: 12.4 us -> 0.01 us  [local(): jnp.stack([speed.reshape(cz, cx * cy), incident[0].reshape(cz, cx * cy)])]
    add x5 -> x1, other arithmetic: 11.1 us -> 0.68 us  [local(): rows_at = ((at_z % cz * cx + at_x % cx) * cy + at_y)[None]]
    concatenate x16 -> x0, other arithmetic: 7.02 us -> none  [the longest x15 6.94 us: with_halo(): jnp.concatenate([lax.ppermute(tail, axis, [(i, (i + 1) % count) for i in...]
    slice x11 -> x0, local copies, waits for them, and re-layouts: 5.6 us -> none  [the longest x5 2.38 us: with_halo(): lax.slice_in_dim(cells, cells.shape[dim] - width, cells.shape[dim], axis=...]
  transfers between devices with their start and end apart: 21 -> 0, of which waited for: 19 -> 0; matrix products, arithmetic and copies ran while one was open for 1% -> 0% of each run, Pallas kernels for 0% -> 0%
where the time goes in v1:
time: 78.9 us; the launch traced here: 78.6 us
  Pallas kernels  72.5 us (92%)
  local copies, waits for them, and re-layouts  4.68 us (6%)
    pallas_call x1, Pallas kernels, local(): pl.pallas_call(functools.partial(kernel, sizes), out_shape=(jax.ShapeDtyp...  72.5 us
    unnamed x10, local copies, waits for them, and re-layouts  3.68 us

profile of v1, /device:TPU:0, one launch (start us, length us, event | category | flops | bytes accessed | tf_op | source)
XLA Modules:
  0.0 78.6 jit_solution(10603077569059630814)
XLA Ops:
  0.6 0.0 copy-start.2
  0.6 0.7 fusion.12.rows_at
  1.3 0.8 %stack_reshape.3 = f32[1,8,128]{2,1,0:T(8,128)S(1)} reshape(f32[8,8,16]{2,1,0:T(8,128)} %param.6) | data formatting | bytes 8192 | tf_op jit(solution)/shard_map/stack;reshape | solution.py:462
  2.2 0.0 copy-done.2
  2.2 0.1 stack_reshape_squeeze.3
  2.2 0.0 copy-start.3
  2.2 0.6 copy-done.3
  2.9 0.1 copy.7
  3.0 0.0 copy-start.1
  3.0 0.1 fusion.6.group_of
  3.1 0.6 copy-done.1
  3.7 0.0 copy-start
  3.7 1.0 %copy-done = f32[8,8,16,128]{3,2,1,0:T(8,128)S(1)} copy-done((f32[8,8,16,128]{3,2,1,0:T(8,128)S(1)}, f32[8,8,16,128]{3,2,1,0:T(8,128)}, u32[]{:S(2)}) %copy-start) | copy-done | bytes 524312
  4.7 72.5 %shard_map.68 = (f32[64,16,128]{2,1,0:T(8,128)S(1)}, f32[128,128]{1,0:T(8,128)S(1)}) custom-call(f32[1,6]{1,0:T(1,128)S(1)} %copy-done.1, s32[1,64]{1,0:T(1,128)S(1)} %fusion.12.rows_at, f32[64,16,128]{2,1,0:T(8,128)S(1)} %bitcast.5, f32[2,8,128]{2,1,0:T(8,128)S(1)} %pad_maximum_fusion.medium, s32[64,1]{1,0:T(8,128)S(1)} %fusion.6.group_of), custom_call_target="tpu_custom_call" | custom-call | tf_op jit(solution)/shard_map/pallas_call | solution.py:474
  77.2 0.8 %copy.13 = f32[1,8,8,16,128]{4,3,2,1,0:T(8,128)} copy(f32[1,8,8,16,128]{4,3,2,1,0:T(8,128)S(1)} %bitcast.6) | data formatting | bytes 1048576
  78.0 0.6 copy.14
  (1 shorter events, 0.0 us)
Async XLA Ops:
  0.6 1.5 %copy-start.2 = (f32[1,8,8,16]{3,2,1,0:T(8,128)S(1)}, f32[1,8,8,16]{3,2,1,0:T(8,128)}, u32[]{:S(2)}) copy-start(f32[1,8,8,16]{3,2,1,0:T(8,128)} %param.7) | copy-start | bytes 12292
  2.2 0.7 copy-start.3
  3.0 0.7 copy-start.1
  3.7 1.0 %copy-start = (f32[8,8,16,128]{3,2,1,0:T(8,128)S(1)}, f32[8,8,16,128]{3,2,1,0:T(8,128)}, u32[]{:S(2)}) copy-start(f32[8,8,16,128]{3,2,1,0:T(8,128)} %param.5) | copy-start | bytes 1572868

commit v2 on v1

--- a/solution.py
+++ b/solution.py
@@ -25,11 +25,12 @@
     sizes,
     wavelet,
     rows_at,
-    probes,
+    probes_at,
     medium,
     group_of,
     out,
     factor,
+    probes,
     fields,
     flat,
     drive,
@@ -40,10 +41,9 @@
     picked,
     out_a,
     in_a,
-    all_a,
-    out_b,
+    partial,
     in_b,
-    all_b,
+    whole,
     core,
     pack_s,
     pack_r,
@@ -53,14 +53,13 @@
     x_r,
     a_s,
     a_r,
-    ba_s,
-    ba_r,
     b_s,
     b_r,
-    bb_s,
-    bb_r,
+    c_s,
+    c_r,
     o_s,
     o_r,
+    probes_s,
 ):
     nz, ns, cz, cx, cy, width, steps, receivers = sizes
     cells = cz * cx
@@ -70,8 +69,9 @@
     everyone = members * ns
     owners = min(members, receivers // 8)
     own_rows = receivers // owners
-    gram_rows = width // owners
-    early = (steps - 1) * own_rows
+    rounds = -(-steps // nz)
+    keepers = min(everyone, width // 8)
+    kept = width // keepers
 
     z = lax.axis_index("gz")
     s = lax.axis_index("shot")
@@ -95,6 +95,8 @@
         tm = t % members
         return ts, tm, tm // 2, tm % 2
 
+    probes_copy = pltpu.make_async_copy(probes_at, probes, probes_s)
+    probes_copy.start()
     barrier = pltpu.get_barrier_semaphore()
 
     def greet(i, c):
@@ -109,38 +111,43 @@
 
     lax.fori_loop(0, everyone - 1, greet, 0)
 
-    def pack(source, zd):
+    def turn(blocks):
+        blocks = list(blocks)
+        half = nz // 2
+        while half:
+            upper = lax.broadcasted_iota(jnp.int32, blocks[0].shape, 1) // (group * half) % 2 == 1
+            for q in range(nz):
+                if q & half:
+                    continue
+                a, b = blocks[q], blocks[q + half]
+                if 2 * half == nz:
+                    mixed = pltpu.roll(jnp.where(upper, a, b), group * half, 1)
+                    blocks[q] = jnp.where(upper, mixed, a)
+                    blocks[q + half] = jnp.where(upper, b, mixed)
+                else:
+                    blocks[q] = jnp.where(upper, pltpu.roll(b, group * half, 1), a)
+                    blocks[q + half] = jnp.where(upper, b, pltpu.roll(a, width - group * half, 1))
+            half //= 2
+        return blocks
+
+    def pack(source):
         def body(c, carry):
-            acc = None
-            for q in range(nz):
-                part_q = source(q * part + c)
-                shift = (group * (q - zd)) % width
-                if shift:
-                    part_q = pltpu.roll(part_q, shift, 1)
-                acc = part_q if acc is None else jnp.where(lanes == q, part_q, acc)
-            send[zd, c] = acc
+            for zd, block in enumerate(turn([source(q * part + c) for q in range(nz)])):
+                send[zd, c] = block
             return carry
 
-        lax.fori_loop(0, part, body, 0, unroll=2)
+        lax.fori_loop(0, part, body, 0, unroll=4)
 
     def unpack(target):
-        for q in range(nz):
-
-            def body(c, carry):
-                acc = None
-                for zs in range(nz):
-                    piece = recv[zs, c]
-                    shift = (group * (zs - q)) % width
-                    if shift:
-                        piece = pltpu.roll(piece, shift, 1)
-                    acc = piece if acc is None else jnp.where(lanes == zs, piece, acc)
-                target(q * part + c, acc)
-                return carry
-
-            lax.fori_loop(0, part, body, 0, unroll=2)
-
-    for zd in range(nz):
-        pack(lambda i: probes[i], zd)
+        def body(c, carry):
+            for q, block in enumerate(turn([recv[zs, c] for zs in range(nz)])):
+                target(q * part + c, block)
+            return carry
+
+        lax.fori_loop(0, part, body, 0, unroll=4)
+
+    probes_copy.wait()
+    pack(lambda i: probes[i])
     pl.semaphore_wait(barrier, everyone - 1)
 
     def exchange_start(ss, rs, land):
@@ -194,9 +201,10 @@
 
         lax.fori_loop(0, cz, clear, 0)
 
-    probe_gram = gram_of(probes[...].reshape(cells * cy, width))
-    for o in range(owners):
-        out_a[o, early : early + gram_rows] = probe_gram[o * gram_rows : (o + 1) * gram_rows]
+    total_cells = float(nz * cz * 2 * cx * cy)
+    count = float(ns * steps * receivers)
+    core[...] = (damping / (ns * total_cells)) * gram_of(probes[...].reshape(cells * cy, width))
+    out_a[...] = jnp.zeros_like(out_a)
 
     media_body(True)
     columns = cx * cy
@@ -220,26 +228,19 @@
 
     low = lanes == 0
     high = lanes == nz - 1
-
-    def put(n, i, j, value):
+    spans = ((0, DEPTH), (DEPTH, cz - DEPTH), (cz - DEPTH, cz))
+
+    def put(n, span, i, j, value):
         flat[pl.ds((i * cx + j) * cy, cy)] = value
         if n < steps - 1:
-            fields[n, DEPTH + i, DEPTH + j, PAD : PAD + cy] = value
-
-    def fold(n):
-        for i in range(DEPTH):
-
-            def body(j, c):
-                rows = pl.ds(PAD, cy)
-                below = fields[n, DEPTH + cz - DEPTH + i, DEPTH + j, rows]
-                above = fields[n, DEPTH + i, DEPTH + j, rows]
-                below = jnp.where(low, 0.0, pltpu.roll(below, group, 1))
-                above = jnp.where(high, 0.0, pltpu.roll(above, width - group, 1))
-                fields[n, i, DEPTH + j, rows] = below
+            rows = pl.ds(PAD, cy)
+            fields[n, DEPTH + i, DEPTH + j, rows] = value
+            if span == 0:
+                above = jnp.where(high, 0.0, pltpu.roll(value, width - group, 1))
                 fields[n, DEPTH + cz + i, DEPTH + j, rows] = above
-                return c
-
-            lax.fori_loop(0, cx, body, 0, unroll=2)
+            if span == 2:
+                below = jnp.where(low, 0.0, pltpu.roll(value, group, 1))
+                fields[n, DEPTH + i - cz, DEPTH + j, rows] = below
 
     near = (cx - DEPTH) * (1 - x)
     far = (cx - DEPTH) - near
@@ -253,7 +254,7 @@
     def advance(n, start):
         amplitude = wavelet[0, n]
 
-        def body(i, c):
+        def body(span, i, c):
             for jj in range(DEPTH):
                 j = start + jj
                 a, b = DEPTH + i, DEPTH + j
@@ -268,10 +269,11 @@
                 value = 2.0 * now + speed[cell] * total + amplitude * drive[cell]
                 if n > 1:
                     value -= fields[n - 2, a, b, PAD : PAD + cy]
-                put(n, i, j, value)
-            return c
-
-        lax.fori_loop(0, cz, body, 0)
+                put(n, span, i, j, value)
+            return c
+
+        for span, (least, most) in enumerate(spans):
+            lax.fori_loop(least, most, functools.partial(body, span), 0)
 
     wide = lax.broadcasted_iota(jnp.int32, (receivers, width), 1) // group
 
@@ -283,122 +285,137 @@
         while shift < width:
             rows = rows + pltpu.roll(rows, shift, 1)
             shift *= 2
-        rows = jnp.where(wide == z, rows, 0.0)
+        rows = jnp.where(wide == n % nz, rows, 0.0)
         for o in range(owners):
-            piece = rows[o * own_rows : (o + 1) * own_rows]
-            if n < steps - 1:
-                out_a[o, n * own_rows : (n + 1) * own_rows] = piece
-            else:
-                out_b[o] = piece
-
-    def only(condition, body):
-        if owners == members:
+            out_a[o, n // nz] += rows[o * own_rows : (o + 1) * own_rows]
+
+    def only(condition, all_do, body):
+        if all_do:
             body()
         else:
             pl.when(condition)(body)
 
-    def to_owners(outgoing, incoming, ss, rs, act):
+    def slabs(act):
+        every = owners == members
+
         def body(i, c):
             t = (m + 1 + i) % members
+            there = (t // 2, s, t % 2)
 
             def start():
-                remote(
-                    outgoing.at[t], incoming.at[m], ss.at[t], rs.at[m], t // 2, s, t % 2
-                ).start()
+                remote(out_a.at[t], in_a.at[m], a_s.at[t], a_r.at[m], *there).start()
 
             def sent():
-                remote(
-                    outgoing.at[t], incoming.at[m], ss.at[t], rs.at[m], t // 2, s, t % 2
-                ).wait_send()
+                remote(out_a.at[t], in_a.at[m], a_s.at[t], a_r.at[m], *there).wait_send()
 
             def arrived():
-                remote(
-                    outgoing.at[0], incoming.at[t], ss.at[t], rs.at[t], t // 2, s, t % 2
-                ).wait_recv()
+                remote(out_a.at[0], in_a.at[t], a_s.at[t], a_r.at[t], *there).wait_recv()
 
             if act == "arrived":
-                only(m < owners, arrived)
+                only(m < owners, every, arrived)
             else:
-                only(t < owners, start if act == "start" else sent)
+                only(t < owners, every, start if act == "start" else sent)
             return c
 
         lax.fori_loop(0, members - 1, body, 0)
 
-    def sum_up(outgoing, incoming, spread):
-        def body():
-            incoming[m] = outgoing[m]
-            total = incoming[0]
-            for t in range(1, members):
-                total = total + incoming[t]
-            spread[s, m] = total
-
-        only(m < owners, body)
-
-    def to_all(spread, ss, rs, act):
+    def scatter(act):
+        every = keepers == everyone
+
         def body(i, c):
             t = (f + 1 + i) % everyone
-            ts, tm, tz, tx = split(t)
+            ts, _, tz, tx = split(t)
 
             def start():
-                remote(spread.at[s, m], spread.at[s, m], ss.at[t], rs.at[f], tz, ts, tx).start()
+                remote(partial.at[t], in_b.at[f], b_s.at[t], b_r.at[f], tz, ts, tx).start()
 
             def sent():
-                remote(spread.at[s, m], spread.at[s, m], ss.at[t], rs.at[f], tz, ts, tx).wait_send()
+                remote(partial.at[t], in_b.at[f], b_s.at[t], b_r.at[f], tz, ts, tx).wait_send()
 
             def arrived():
-                remote(spread.at[ts, tm], spread.at[ts, tm], ss.at[t], rs.at[t], tz, ts, tx).wait_recv()
+                remote(partial.at[0], in_b.at[t], b_s.at[t], b_r.at[t], tz, ts, tx).wait_recv()
 
             if act == "arrived":
-                only(tm < owners, arrived)
+                only(f < keepers, every, arrived)
             else:
-                only(m < owners, start if act == "start" else sent)
+                only(t < keepers, every, start if act == "start" else sent)
             return c
 
         lax.fori_loop(0, everyone - 1, body, 0)
 
+    def gather(act):
+        every = keepers == everyone
+
+        def body(i, c):
+            t = (f + 1 + i) % everyone
+            ts, _, tz, tx = split(t)
+
+            def start():
+                remote(whole.at[f], whole.at[f], c_s.at[t], c_r.at[f], tz, ts, tx).start()
+
+            def sent():
+                remote(whole.at[f], whole.at[f], c_s.at[t], c_r.at[f], tz, ts, tx).wait_send()
+
+            def arrived():
+                remote(whole.at[t], whole.at[t], c_s.at[t], c_r.at[t], tz, ts, tx).wait_recv()
+
+            if act == "arrived":
+                only(t < keepers, every, arrived)
+            else:
+                only(f < keepers, every, start if act == "start" else sent)
+            return c
+
+        lax.fori_loop(0, everyone - 1, body, 0)
+
     first = wavelet[0, 0]
 
-    def begin(i, c):
+    def begin(span, i, c):
         for j in range(cx):
-            put(0, i, j, first * drive[i * cx + j])
+            put(0, span, i, j, first * drive[i * cx + j])
         return c
 
-    lax.fori_loop(0, cz, begin, 0)
+    for span, (least, most) in enumerate(spans):
+        lax.fori_loop(least, most, functools.partial(begin, span), 0)
     border(0, False).start()
-    fold(0)
     pick(0)
     for n in range(1, steps):
         advance(n, far)
-        if n == steps - 1:
-            to_owners(out_a, in_a, a_s, a_r, "arrived")
-            sum_up(out_a, in_a, all_a)
-            to_all(all_a, ba_s, ba_r, "start")
         border(n - 1, True).wait_recv()
         advance(n, near)
         if n < steps - 1:
             border(n, False).start()
-            fold(n)
         pick(n)
-        if n == steps - 2:
-            to_owners(out_a, in_a, a_s, a_r, "start")
-    to_owners(out_b, in_b, b_s, b_r, "start")
-    for zd in range(nz):
-        pack(lambda i: flat[pl.ds(pl.multiple_of(i * cy, cy), cy)], zd)
-    to_owners(out_b, in_b, b_s, b_r, "arrived")
-    sum_up(out_b, in_b, all_b)
-    to_all(all_b, bb_s, bb_r, "start")
-
-    to_all(all_a, ba_s, ba_r, "arrived")
-    sampled = all_a[:, :, 0:early].reshape(ns * owners * early, width)
-    probe_part = jnp.zeros((width, width), F32)
-    probe_part = all_a[s, :, early : early + gram_rows].reshape(width, width)
-    total_cells = float(nz * cz * 2 * cx * cy)
-    count = float(ns * steps * receivers)
-    core[...] = gram_of(sampled) / count + damping * probe_part / total_cells
-    to_all(all_b, bb_s, bb_r, "arrived")
+    slabs("start")
+    pack(lambda i: flat[pl.ds(pl.multiple_of(i * cy, cy), cy)])
+    slabs("arrived")
+
+    def own_part():
+        in_a[m] = out_a[m]
+        total = core[...]
+        for h in range(rounds):
+            held = turn([in_a[2 * q, h] + in_a[2 * q + 1, h] for q in range(nz)])
+            total += gram_of(jnp.concatenate(held, axis=0)) / count
+        core[...] = total
+
+    only(m < owners, owners == members, own_part)
+    for k in range(keepers):
+        partial[k] = core[k * kept : (k + 1) * kept]
+    scatter("start")
+    scatter("arrived")
+
+    def keep():
+        in_b[f] = partial[f]
+        total = in_b[0]
+        for t in range(1, everyone):
+            total = total + in_b[t]
+        whole[f] = total
+
+    only(f < keepers, keepers == everyone, keep)
+    gather("start")
+    gather("arrived")
     exchange_start(o_s, o_r, recv)
     recv[z] = send[z]
-    core[...] += gram_of(all_b[...].reshape(ns * owners * own_rows, width)) / count
+    core[...] = whole[...].reshape(width, width)
 
     panel = 8
     row_in = lax.broadcasted_iota(jnp.int32, (panel, width), 0)
@@ -438,10 +455,9 @@
 
     for n in range(steps - 1):
         border(n, False).wait_send()
-    to_owners(out_a, in_a, a_s, a_r, "sent")
-    to_owners(out_b, in_b, b_s, b_r, "sent")
-    to_all(all_a, ba_s, ba_r, "sent")
-    to_all(all_b, bb_s, bb_r, "sent")
+    slabs("sent")
+    scatter("sent")
+    gather("sent")
 
 
 def local(probes, speed, incident, wavelet, receivers):
@@ -465,7 +481,8 @@
     everyone = members * ns
     owners = min(members, count // 8)
     own_rows = count // owners
-    message = (steps - 1) * own_rows + width // owners
+    rounds = -(-steps // nz)
+    keepers = min(everyone, width // 8)
     part = cells // nz
     dma = pltpu.SemaphoreType.DMA
     vmem = pl.BlockSpec(memory_space=pltpu.VMEM)
@@ -477,9 +494,10 @@
             jax.ShapeDtypeStruct((cells, cy, width), F32),
             jax.ShapeDtypeStruct((width, width), F32),
         ),
-        in_specs=[smem, smem, vmem, vmem, vmem],
+        in_specs=[smem, smem, pl.BlockSpec(memory_space=pl.ANY), vmem, vmem],
         out_specs=(vmem, vmem),
         scratch_shapes=[
+            pltpu.VMEM((cells, cy, width), F32),
             pltpu.VMEM((steps - 1, cz + 2 * DEPTH, cx + 2 * DEPTH, cy + 2 * PAD, width), F32),
             pltpu.VMEM((cells * cy, width), F32),
             pltpu.VMEM((cells, cy, width), F32),
@@ -488,12 +506,11 @@
             pltpu.VMEM((nz, part, cy, width), F32),
             pltpu.VMEM((nz, 2, cz, cx * cy), F32),
             pltpu.VMEM((count, width), F32),
-            pltpu.VMEM((owners, message, width), F32),
-            pltpu.VMEM((members, message, width), F32),
-            pltpu.VMEM((ns, owners, message, width), F32),
-            pltpu.VMEM((owners, own_rows, width), F32),
-            pltpu.VMEM((members, own_rows, width), F32),
-            pltpu.VMEM((ns, owners, own_rows, width), F32),
+            pltpu.VMEM((owners, rounds, own_rows, width), F32),
+            pltpu.VMEM((members, rounds, own_rows, width), F32),
+            pltpu.VMEM((keepers, width // keepers, width), F32),
+            pltpu.VMEM((everyone, width // keepers, width), F32),
+            pltpu.VMEM((keepers, width // keepers, width), F32),
             pltpu.VMEM((width, width), F32),
             dma((nz,)),
             dma((nz,)),
@@ -505,12 +522,11 @@
             dma((members,)),
             dma((everyone,)),
             dma((everyone,)),
-            dma((members,)),
-            dma((members,)),
             dma((everyone,)),
             dma((everyone,)),
             dma((nz,)),
             dma((nz,)),
+            dma,
         ],
         compiler_params=pltpu.CompilerParams(
             collective_id=0, has_side_effects=True, vmem_limit_bytes=48 * 1024 * 1024

time: 78.9 us -> 72.5 us (0.919)
  Pallas kernels: 72.5 us -> 66.1 us
    pallas_call x1, Pallas kernels: 72.5 us -> 66.1 us  [local(): pl.pallas_call(functools.partial(kernel, sizes), out_shape=(jax.ShapeDtyp...]
where the time goes in v2:
time: 72.5 us; the launch traced here: 72.2 us
  Pallas kernels  66.1 us (91%)
  local copies, waits for them, and re-layouts  4.68 us (6%)
  other arithmetic  0.78 us (1%)
    pallas_call x1, Pallas kernels, local(): pl.pallas_call(functools.partial(kernel, sizes), out_shape=(jax.ShapeDtyp...  66.1 us
    unnamed x10, local copies, waits for them, and re-layouts  3.68 us

profile of v2, /device:TPU:0, one launch (start us, length us, event | category | flops | bytes accessed | tf_op | source)
XLA Modules:
  0.0 72.2 jit_solution(5132953045454463835)
XLA Ops:
  0.6 0.0 copy-start.2
  0.6 0.7 fusion.12.rows_at
  1.3 0.8 %stack_reshape.3 = f32[1,8,128]{2,1,0:T(8,128)S(1)} reshape(f32[8,8,16]{2,1,0:T(8,128)} %param.6) | data formatting | bytes 8192 | tf_op jit(solution)/shard_map/stack;reshape | solution.py:478
  2.2 0.0 copy-done.2
  2.2 0.1 stack_reshape_squeeze.3
  2.2 0.0 copy-start.3
  2.2 0.6 copy-done.3
  2.9 0.1 copy.7
  3.0 0.0 copy-start.1
  3.0 0.1 fusion.6.group_of
  3.1 0.6 copy-done.1
  3.7 0.0 copy-start
  3.7 1.0 %copy-done = f32[8,8,16,128]{3,2,1,0:T(8,128)S(1)} copy-done((f32[8,8,16,128]{3,2,1,0:T(8,128)S(1)}, f32[8,8,16,128]{3,2,1,0:T(8,128)}, u32[]{:S(2)}) %copy-start) | copy-done | bytes 524312
  4.7 66.1 %shard_map.68 = (f32[64,16,128]{2,1,0:T(8,128)S(1)}, f32[128,128]{1,0:T(8,128)S(1)}) custom-call(f32[1,6]{1,0:T(1,128)S(1)} %copy-done.1, s32[1,64]{1,0:T(1,128)S(1)} %fusion.12.rows_at, f32[64,16,128]{2,1,0:T(8,128)S(1)} %bitcast.5, f32[2,8,128]{2,1,0:T(8,128)S(1)} %pad_maximum_fusion.medium, s32[64,1]{1,0:T(8,128)S(1)} %fusion.6.group_of), custom_call_target="tpu_custom_call" | custom-call | tf_op jit(solution)/shard_map/pallas_call | solution.py:491
  70.8 0.8 %copy.13 = f32[1,8,8,16,128]{4,3,2,1,0:T(8,128)} copy(f32[1,8,8,16,128]{4,3,2,1,0:T(8,128)S(1)} %bitcast.6) | data formatting | bytes 1048576
  71.6 0.6 copy.14
  (1 shorter events, 0.0 us)
Async XLA Ops:
  0.6 1.5 %copy-start.2 = (f32[1,8,8,16]{3,2,1,0:T(8,128)S(1)}, f32[1,8,8,16]{3,2,1,0:T(8,128)}, u32[]{:S(2)}) copy-start(f32[1,8,8,16]{3,2,1,0:T(8,128)} %param.7) | copy-start | bytes 12292
  2.2 0.7 copy-start.3
  3.0 0.7 copy-start.1
  3.7 1.0 %copy-start = (f32[8,8,16,128]{3,2,1,0:T(8,128)S(1)}, f32[8,8,16,128]{3,2,1,0:T(8,128)}, u32[]{:S(2)}) copy-start(f32[8,8,16,128]{3,2,1,0:T(8,128)} %param.5) | copy-start | bytes 1572868

commit v3 on v2

--- a/solution.py
+++ b/solution.py
@@ -90,26 +90,39 @@
             device_id_type=pl.DeviceIdType.MESH,
         )
 
-    def split(t):
-        ts = t // members
-        tm = t % members
-        return ts, tm, tm // 2, tm % 2
+    def partners(shots, body):
+        def at(tz, near):
+            for ds in range(ns if shots else 1):
+                ts = lax.rem(s + ds, ns) if ds else s
+                for dx in range(2):
+                    if ds or dx or not near:
+                        body(tz, ts, 1 - x if dx else x)
+
+        if nz <= 4:
+            for dz in range(1, nz):
+                at(lax.rem(z + dz, nz), False)
+        else:
+
+            def step(dz, c):
+                at(lax.rem(z + dz, nz), False)
+                return c
+
+            lax.fori_loop(1, nz, step, 0)
+        at(z, True)
 
     probes_copy = pltpu.make_async_copy(probes_at, probes, probes_s)
     probes_copy.start()
     barrier = pltpu.get_barrier_semaphore()
 
-    def greet(i, c):
-        ts, _, tz, tx = split((f + 1 + i) % everyone)
+    def greet(tz, ts, tx):
         pl.semaphore_signal(
             barrier,
             inc=1,
             device_id={"gz": tz, "shot": ts, "gx": tx},
             device_id_type=pl.DeviceIdType.MESH,
         )
-        return c
-
-    lax.fori_loop(0, everyone - 1, greet, 0)
+
+    partners(True, greet)
 
     def turn(blocks):
         blocks = list(blocks)
@@ -150,25 +163,24 @@
     pack(lambda i: probes[i])
     pl.semaphore_wait(barrier, everyone - 1)
 
+    def along(body):
+        for dz in range(1, nz):
+            body(lax.rem(z + dz, nz))
+
     def exchange_start(ss, rs, land):
-        def body(i, c):
-            tz = (z + 1 + i) % nz
+        def body(tz):
             remote(send.at[tz], land.at[z], ss.at[tz], rs.at[z], tz, s, x).start()
-            return c
-
-        lax.fori_loop(0, nz - 1, body, 0)
+
+        along(body)
 
     def exchange_wait(ss, rs, land):
-        def body(i, c):
-            tz = (z + 1 + i) % nz
+        def body(tz):
             remote(send.at[tz], land.at[tz], ss.at[tz], rs.at[tz], tz, s, x).wait()
-            return c
-
-        lax.fori_loop(0, nz - 1, body, 0)
+
+        along(body)
 
     def media_body(wait):
-        def body(i, c):
-            tz = (z + 1 + i) % nz
+        def body(tz):
             here = media.at[tz] if wait else media.at[z]
             copy = remote(
                 medium, here, med_s.at[tz], med_r.at[tz if wait else z], tz, s, x
@@ -177,9 +189,8 @@
                 copy.wait()
             else:
                 copy.start()
-            return c
-
-        lax.fori_loop(0, nz - 1, body, 0)
+
+        along(body)
 
     media_body(False)
     exchange_start(pack_s, pack_r, recv)
@@ -298,9 +309,8 @@
     def slabs(act):
         every = owners == members
 
-        def body(i, c):
-            t = (m + 1 + i) % members
-            there = (t // 2, s, t % 2)
+        def body(*there):
+            t = there[0] * 2 + there[2]
 
             def start():
                 remote(out_a.at[t], in_a.at[m], a_s.at[t], a_r.at[m], *there).start()
@@ -315,16 +325,14 @@
                 only(m < owners, every, arrived)
             else:
                 only(t < owners, every, start if act == "start" else sent)
-            return c
-
-        lax.fori_loop(0, members - 1, body, 0)
+
+        partners(False, body)
 
     def scatter(act):
         every = keepers == everyone
 
-        def body(i, c):
-            t = (f + 1 + i) % everyone
-            ts, _, tz, tx = split(t)
+        def body(tz, ts, tx):
+            t = ts * members + tz * 2 + tx
 
             def start():
                 remote(partial.at[t], in_b.at[f], b_s.at[t], b_r.at[f], tz, ts, tx).start()
@@ -339,16 +347,14 @@
                 only(f < keepers, every, arrived)
             else:
                 only(t < keepers, every, start if act == "start" else sent)
-            return c
-
-        lax.fori_loop(0, everyone - 1, body, 0)
+
+        partners(True, body)
 
     def gather(act):
         every = keepers == everyone
 
-        def body(i, c):
-            t = (f + 1 + i) % everyone
-            ts, _, tz, tx = split(t)
+        def body(tz, ts, tx):
+            t = ts * members + tz * 2 + tx
 
             def start():
                 remote(whole.at[f], whole.at[f], c_s.at[t], c_r.at[f], tz, ts, tx).start()
@@ -363,9 +369,8 @@
                 only(t < keepers, every, arrived)
             else:
                 only(f < keepers, every, start if act == "start" else sent)
-            return c
-
-        lax.fori_loop(0, everyone - 1, body, 0)
+
+        partners(True, body)
 
     first = wavelet[0, 0]
 
@@ -412,9 +417,9 @@
 
     only(f < keepers, keepers == everyone, keep)
     gather("start")
-    gather("arrived")
     exchange_start(o_s, o_r, recv)
     recv[z] = send[z]
+    gather("arrived")
     core[...] = whole[...].reshape(width, width)
 
     panel = 8

time: 72.5 us -> 69.1 us (0.953)
  Pallas kernels: 66.1 us -> 62.6 us
    pallas_call x1, Pallas kernels: 66.1 us -> 62.6 us  [local(): pl.pallas_call(functools.partial(kernel, sizes), out_shape=(jax.ShapeDtyp...]
where the time goes in v3:
time: 69.1 us; the launch traced here: 68.8 us
  Pallas kernels  62.6 us (91%)
  local copies, waits for them, and re-layouts  4.68 us (7%)
  other arithmetic  0.78 us (1%)
    pallas_call x1, Pallas kernels, local(): pl.pallas_call(functools.partial(kernel, sizes), out_shape=(jax.ShapeDtyp...  62.6 us
    unnamed x10, local copies, waits for them, and re-layouts  3.68 us

profile of v3, /device:TPU:0, one launch (start us, length us, event | category | flops | bytes accessed | tf_op | source)
XLA Modules:
  0.0 68.8 jit_solution(3211189965034063095)
XLA Ops:
  0.6 0.0 copy-start.2
  0.6 0.7 fusion.12.rows_at
  1.3 0.8 %stack_reshape.3 = f32[1,8,128]{2,1,0:T(8,128)S(1)} reshape(f32[8,8,16]{2,1,0:T(8,128)} %param.6) | data formatting | bytes 8192 | tf_op jit(solution)/shard_map/stack;reshape | solution.py:483
  2.2 0.0 copy-done.2
  2.2 0.1 stack_reshape_squeeze.3
  2.2 0.0 copy-start.3
  2.2 0.6 copy-done.3
  2.9 0.1 copy.7
  3.0 0.0 copy-start.1
  3.0 0.1 fusion.6.group_of
  3.1 0.6 copy-done.1
  3.7 0.0 copy-start
  3.7 1.0 %copy-done = f32[8,8,16,128]{3,2,1,0:T(8,128)S(1)} copy-done((f32[8,8,16,128]{3,2,1,0:T(8,128)S(1)}, f32[8,8,16,128]{3,2,1,0:T(8,128)}, u32[]{:S(2)}) %copy-start) | copy-done | bytes 524312
  4.7 62.6 %shard_map.68 = (f32[64,16,128]{2,1,0:T(8,128)S(1)}, f32[128,128]{1,0:T(8,128)S(1)}) custom-call(f32[1,6]{1,0:T(1,128)S(1)} %copy-done.1, s32[1,64]{1,0:T(1,128)S(1)} %fusion.12.rows_at, f32[64,16,128]{2,1,0:T(8,128)S(1)} %bitcast.5, f32[2,8,128]{2,1,0:T(8,128)S(1)} %pad_maximum_fusion.medium, s32[64,1]{1,0:T(8,128)S(1)} %fusion.6.group_of), custom_call_target="tpu_custom_call" | custom-call | tf_op jit(solution)/shard_map/pallas_call | solution.py:496
  67.3 0.8 %copy.13 = f32[1,8,8,16,128]{4,3,2,1,0:T(8,128)} copy(f32[1,8,8,16,128]{4,3,2,1,0:T(8,128)S(1)} %bitcast.6) | data formatting | bytes 1048576
  68.1 0.6 copy.14
  (1 shorter events, 0.0 us)
Async XLA Ops:
  0.6 1.5 %copy-start.2 = (f32[1,8,8,16]{3,2,1,0:T(8,128)S(1)}, f32[1,8,8,16]{3,2,1,0:T(8,128)}, u32[]{:S(2)}) copy-start(f32[1,8,8,16]{3,2,1,0:T(8,128)} %param.7) | copy-start | bytes 12292
  2.2 0.7 copy-start.3
  3.0 0.7 copy-start.1
  3.7 1.0 %copy-start = (f32[8,8,16,128]{3,2,1,0:T(8,128)S(1)}, f32[8,8,16,128]{3,2,1,0:T(8,128)}, u32[]{:S(2)}) copy-start(f32[8,8,16,128]{3,2,1,0:T(8,128)} %param.5) | copy-start | bytes 1572868
